TPU v7x, 128 devices: a whole 4x4x4 slice. The times are simulated.
128 devices in a mesh: wide: 16 (over z_hi, y, core), narrow: 8 (over z_lo, x).
Axes of the slice: x: 4, y: 4, z: 4 (z_hi: 2, z_lo: 2; z = z_hi * 2 + z_lo), core: 2. Of those that a mesh axis runs over, the one named last changes fastest.
Arguments:
- state: float32 [16, 8, 524288], P('wide', 'narrow'), may hold values from -6 to 6
- angles: float32 [6, 2, 7], replicated, may hold values from -3.140625 to 3.140625
- cz_pairs: int32 [6, 12, 2], replicated, may hold values from 0 to 18
Outputs:
- final_state: float32 [16, 8, 524288], P('wide', 'narrow')
All inputs are finite; a program needn't handle non-finite values.
Results may differ from a plain program's by a relative error of at most 0.0003.
Values sent between devices are 32-bit elements; how exact they have to be, the bound alone decides.
A program may use at most 64 MiB of HBM per device.

v0:
```python
import functools

import jax
import jax.numpy as jnp
from jax import lax
from jax.experimental import pallas as pl
from jax.experimental.pallas import tpu as pltpu
from jax.sharding import PartitionSpec as P

MESH = pl.DeviceIdType.MESH
F32 = jnp.float32
BF16 = jnp.bfloat16
ROUNDS = 6
ROWS = 128
LANES = 128
HALF = 64
CHUNKS = 32
GROUP = 2
GROUPS = CHUNKS // GROUP
LAG = 1


def trade_bit(k, wide, narrow):
    level = k // 2
    step = jnp.where(level == 0, 1, jnp.where(level == 1, 2, 4))
    index = jnp.where(k % 2 == 0, wide, narrow)
    return step, (index // step) % 2


def partner_of(k, wide, narrow):
    step, bit = trade_bit(k, wide, narrow)
    move = step * (1 - 2 * bit)
    even = 1 - k % 2
    return wide + move * even, narrow + move * (1 - even)


def row_order(pos, k, bit):
    low = pos & 63
    under = low & ((1 << k) - 1)
    over = (low >> k) << (k + 1)
    return under | over | (((pos >> 6) ^ bit) << k)


def fold_parity(bits):
    bits = bits ^ (bits >> 4)
    bits = bits ^ (bits >> 2)
    bits = bits ^ (bits >> 1)
    return bits & 1


def rotation_product(out, inp, cosines, sines, base):
    differ = out ^ inp
    value = 1 - 2 * fold_parity(inp & ~out & 127).astype(F32)
    for qubit in range(7):
        row = base + qubit
        value = value * jnp.where((differ >> qubit) & 1 == 0, cosines[row : row + 1], sines[row : row + 1])
    return value


def split(value):
    high = value.astype(BF16)
    low = (value - high.astype(F32)).astype(BF16)
    return high, low


def iota(shape, axis):
    return lax.broadcasted_iota(jnp.int32, shape, axis)


def build(k, wide, narrow, angles, pairs, right_tab, left_tab, sign_tab, row_tab, lane_tab):
    _, bit = trade_bit(k, wide, narrow)
    before = jnp.maximum(k - 1, 0)
    _, bit_before = trade_bit(before, wide, narrow)
    rows = iota((ROWS, LANES), 0)
    cols = iota((ROWS, LANES), 1)
    slot = iota((16, LANES), 0)
    half = jnp.zeros((16, LANES), F32)
    for block in range(2):
        for qubit in range(7):
            half = jnp.where(slot == block * 8 + qubit, angles[k, block, qubit] * 0.5, half)
    cosines = jnp.cos(half)
    sines = jnp.sin(half)

    high, low = split(rotation_product(cols, rows, cosines, sines, 0))
    both = jnp.concatenate([high, low], axis=1)
    right_tab[k, 0:ROWS, :] = both
    right_tab[k, ROWS : 2 * ROWS, :] = both

    out = row_order(rows, k, bit)
    inp = jnp.where(k == 0, cols, row_order(cols, before, bit_before))
    high, low = split(rotation_product(out, inp, cosines, sines, 8))
    left_tab[k, 0:ROWS, :] = jnp.concatenate([high, high], axis=1)
    left_tab[k, ROWS : 2 * ROWS, :] = jnp.concatenate([low, low], axis=1)

    def signs(index):
        parity = jnp.zeros(index.shape, jnp.int32)
        for pair in range(12):
            parity = parity ^ ((index >> pairs[k, pair, 0]) & (index >> pairs[k, pair, 1]))
        return (1 - 2 * (parity & 1)).astype(F32)

    sign_tab[k] = signs(out * 128 + cols)
    by_row = signs(out[:, :CHUNKS] * 128 + cols[:, :CHUNKS] * 16384)
    row_tab[k] = (by_row * by_row[:, 0:1]).astype(BF16)
    by_lane = signs(rows[:CHUNKS] * 16384 + cols[:CHUNKS])
    lane_tab[k] = by_lane * by_lane[0:1, :] * by_lane[:, 0:1]


def work(k, g, held, leave, right_tab, left_tab, sign_tab, row_tab, lane_tab):
    first = g * GROUP
    chunk = iota((CHUNKS, LANES), 0)
    lanes = lane_tab[k]
    picks = jnp.concatenate(
        [jnp.where(chunk == first + j, lanes, 0.0) for j in range(GROUP)], axis=1
    ).astype(BF16)
    phase = jnp.dot(row_tab[k], picks, preferred_element_type=F32)
    sign = sign_tab[k]
    results = []
    for j in range(0, GROUP, 2):
        values = held[k, pl.ds(first + j, 2)].reshape(2 * ROWS, LANES)
        high, low = split(values)
        sums = jnp.dot(jnp.concatenate([high, low], axis=1), right_tab[k], preferred_element_type=F32)
        values = sums[:, :LANES] + sums[:, LANES:]
        high, low = split(values)
        stacked = jnp.concatenate(
            [
                jnp.concatenate([high[:ROWS], high[ROWS:]], axis=1),
                jnp.concatenate([low[:ROWS], low[ROWS:]], axis=1),
            ],
            axis=0,
        )
        sums = jnp.dot(left_tab[k], stacked, preferred_element_type=F32)
        sums = sums[:ROWS] + sums[ROWS:]
        for i in range(2):
            part = slice(i * LANES, (i + 1) * LANES)
            results.append(sums[:, part] * (sign * phase[:, (j + i) * LANES : (j + i + 1) * LANES]))
    for j in range(GROUP):
        held[k + 1, first + j, 0:HALF] = results[j][:HALF]
        leave[k, first + j] = results[j][HALF:]


def kernel(
    angles, pairs, state, final, held, leave, right_tab, left_tab, sign_tab, row_tab, lane_tab, in_sem, out_sem, send_sem, recv_sem
):
    wide = lax.axis_index("wide")
    narrow = lax.axis_index("narrow")
    tables = (right_tab, left_tab, sign_tab, row_tab, lane_tab)

    def fetch(g):
        part = pl.ds(g * GROUP, GROUP)
        return pltpu.make_async_copy(state.at[part], held.at[0, part], in_sem.at[g])

    def trade(k, g):
        part = pl.ds(g * GROUP, GROUP)
        return pltpu.make_async_remote_copy(
            src_ref=leave.at[k, part],
            dst_ref=held.at[k + 1, part, HALF:ROWS],
            send_sem=send_sem.at[k],
            recv_sem=recv_sem.at[k, g],
            device_id=partner_of(k, wide, narrow),
            device_id_type=MESH,
        )

    _, last_bit = trade_bit(jnp.int32(ROUNDS - 1), wide, narrow)

    def deliver(g, side):
        part = pl.ds(g * GROUP, GROUP)
        copies = []
        for upper in range(2):
            begin = side * HALF + upper * 32
            place = upper * HALF + 32 * (last_bit * (1 - 2 * side) + side)
            copies.append(
                pltpu.make_async_copy(
                    held.at[ROUNDS, part, begin : begin + 32],
                    final.at[part, pl.ds(pl.multiple_of(place, 32), 32)],
                    out_sem,
                )
            )
        return copies

    barrier = pltpu.get_barrier_semaphore()
    for k in range(ROUNDS):
        pl.semaphore_signal(barrier, inc=1, device_id=partner_of(jnp.int32(k), wide, narrow), device_id_type=MESH)

    @pl.loop(0, GROUPS)
    def _(g):
        fetch(g).start()

    build(jnp.int32(0), wide, narrow, angles, pairs, *tables)
    pl.semaphore_wait(barrier, ROUNDS)

    @pl.loop(0, GROUPS + ROUNDS * LAG)
    def _(step):
        @pl.loop(0, ROUNDS)
        def _(k):
            g = step - k * LAG

            @pl.when((g >= 0) & (g < GROUPS))
            def _():
                @pl.when(k == 0)
                def _():
                    fetch(g).wait()

                @pl.when(k > 0)
                def _():
                    trade(jnp.maximum(k - 1, 0), g).wait_recv()

                work(k, g, held, leave, *tables)
                trade(k, g).start()

                @pl.when(k == ROUNDS - 1)
                def _():
                    for copy in deliver(g, 0):
                        copy.start()

                @pl.when((g == 0) & (k < ROUNDS - 1))
                def _():
                    build(jnp.minimum(k + 1, ROUNDS - 1), wide, narrow, angles, pairs, *tables)

        done = step - ROUNDS * LAG

        @pl.when(done >= 0)
        def _():
            trade(ROUNDS - 1, done).wait_recv()
            for copy in deliver(done, 1):
                copy.start()

    for k in range(ROUNDS):
        pltpu.make_async_remote_copy(
            src_ref=leave.at[k],
            dst_ref=held.at[k + 1, :, HALF:ROWS],
            send_sem=send_sem.at[k],
            recv_sem=recv_sem.at[k, 0],
            device_id=partner_of(jnp.int32(k), wide, narrow),
            device_id_type=MESH,
        ).wait_send()
    pltpu.make_async_copy(held.at[ROUNDS], final, out_sem).wait()


def body(state, angles, cz_pairs):
    smem = pl.BlockSpec(memory_space=pltpu.SMEM)
    hbm = pl.BlockSpec(memory_space=pl.ANY)
    result = pl.pallas_call(
        kernel,
        out_shape=jax.ShapeDtypeStruct((CHUNKS, ROWS, LANES), F32),
        in_specs=[smem, smem, hbm],
        out_specs=hbm,
        scratch_shapes=[
            pltpu.VMEM((ROUNDS + 1, CHUNKS, ROWS, LANES), F32),
            pltpu.VMEM((ROUNDS, CHUNKS, HALF, LANES), F32),
            pltpu.VMEM((ROUNDS, 2 * ROWS, 2 * LANES), BF16),
            pltpu.VMEM((ROUNDS, 2 * ROWS, 2 * LANES), BF16),
            pltpu.VMEM((ROUNDS, ROWS, LANES), F32),
            pltpu.VMEM((ROUNDS, ROWS, CHUNKS), BF16),
            pltpu.VMEM((ROUNDS, CHUNKS, LANES), F32),
            pltpu.SemaphoreType.DMA((GROUPS,)),
            pltpu.SemaphoreType.DMA,
            pltpu.SemaphoreType.DMA((ROUNDS,)),
            pltpu.SemaphoreType.DMA((ROUNDS, GROUPS)),
        ],
        compiler_params=pltpu.CompilerParams(
            collective_id=0, has_side_effects=True, vmem_limit_bytes=48 << 20
        ),
        name="circuit",
    )(angles, cz_pairs, state.reshape(CHUNKS, ROWS, LANES))
    return result.reshape(state.shape)


def solution(mesh):
    return jax.shard_map(
        body,
        mesh=mesh,
        in_specs=(P("wide", "narrow", None), P(), P()),
        out_specs=P("wide", "narrow", None),
        check_vma=False,
    )
```

profile of v0, /device:TPU:0, one launch (start us, length us, event | category | flops | bytes accessed | tf_op | source)
XLA Modules:
  0.0 93.7 jit_solution(7304218081761965775)
XLA Ops:
  0.0 0.8 copy.4.pairs
  0.8 0.0 copy-start
  0.8 1.6 %copy-done = f32[1,1,524288]{2,1,0:T(1,128)S(1)} copy-done((f32[1,1,524288]{2,1,0:T(1,128)S(1)}, f32[1,1,524288]{2,1,0:T(1,128)}, u32[]{:S(2)}) %copy-start) | copy-done | bytes 2097176
  2.4 0.0 copy-start.1
  2.4 0.7 copy-done.1
  3.1 89.3 %circuit.1 = f32[32,128,128]{2,1,0:T(8,128)S(1)} custom-call(f32[6,2,7]{2,1,0:T(2,128)S(1)} %copy-done.1, s32[6,12,2]{2,1,0:T(8,128)S(1)} %copy.4.pairs, f32[32,128,128]{2,1,0:T(8,128)S(1)} %bitcast.3), custom_call_target="tpu_custom_call" | custom-call | tf_op jit(solution)/shard_map/circuit/pallas_call | solution.py:242
  92.4 1.3 %copy.6 = f32[1,1,524288]{2,1,0:T(1,128)} copy(f32[1,1,524288]{2,1,0:T(1,128)S(1)} %bitcast.2) | data formatting | bytes 4194304
Async XLA Ops:
  0.8 1.6 %copy-start = (f32[1,1,524288]{2,1,0:T(1,128)S(1)}, f32[1,1,524288]{2,1,0:T(1,128)}, u32[]{:S(2)}) copy-start(f32[1,1,524288]{2,1,0:T(1,128)} %param.3) | copy-start | bytes 6291460
  2.4 0.7 copy-start.1
where the time goes:
time: 93.9 us; the launch traced here: 93.7 us
  Pallas kernels  89.3 us (95%)
  local copies, waits for them, and re-layouts  4.41 us (5%)
    pallas_call x1, Pallas kernels, body(): pl.pallas_call(kernel, out_shape=jax.ShapeDtypeStruct((CHUNKS, ROWS, LANE...  89.3 us
    unnamed x6, local copies, waits for them, and re-layouts  4.41 us

commit v1 on v0

v1 whole, which is shorter than its diff:
```python
import functools

import jax
import jax.numpy as jnp
from jax import lax
from jax.experimental import pallas as pl
from jax.experimental.pallas import tpu as pltpu
from jax.sharding import PartitionSpec as P

MESH = pl.DeviceIdType.MESH
F32 = jnp.float32
BF16 = jnp.bfloat16
ROUNDS = 6
ROWS = 128
LANES = 128
HALF = 64
CHUNKS = 32
GROUP = 2
GROUPS = CHUNKS // GROUP
OFFSET = (0, 1, 4, 7, 11, 15, 18)
BLOCKS = (tuple(range(ROUNDS)),)


def trade_bit(k, wide, narrow):
    level = k // 2
    if isinstance(k, int):
        step, index = 1 << level, (narrow if k % 2 else wide)
    else:
        step = jnp.where(level == 0, 1, jnp.where(level == 1, 2, 4))
        index = jnp.where(k % 2 == 0, wide, narrow)
    return step, (index // step) % 2


def partner_of(k, wide, narrow):
    step, bit = trade_bit(k, wide, narrow)
    move = step * (1 - 2 * bit)
    even = 1 - k % 2
    return wide + move * even, narrow + move * (1 - even)


def row_order(pos, k, bit):
    low = pos & 63
    under = low & ((1 << k) - 1)
    over = (low >> k) << (k + 1)
    return under | over | (((pos >> 6) ^ bit) << k)


def fold_parity(bits):
    bits = bits ^ (bits >> 4)
    bits = bits ^ (bits >> 2)
    bits = bits ^ (bits >> 1)
    return bits & 1


def rotation_product(out, inp, cosines, sines, base):
    differ = out ^ inp
    value = 1 - 2 * fold_parity(inp & ~out & 127).astype(F32)
    for qubit in range(7):
        row = base + qubit
        value = value * jnp.where((differ >> qubit) & 1 == 0, cosines[row : row + 1], sines[row : row + 1])
    return value


def split(value):
    high = value.astype(BF16)
    low = (value - high.astype(F32)).astype(BF16)
    return high, low


def iota(shape, axis):
    return lax.broadcasted_iota(jnp.int32, shape, axis)


def build(k, wide, narrow, angles, pairs, right_tab, left_tab, sign_tab, row_tab, lane_tab):
    _, bit = trade_bit(k, wide, narrow)
    before = jnp.maximum(k - 1, 0)
    _, bit_before = trade_bit(before, wide, narrow)
    rows = iota((ROWS, LANES), 0)
    cols = iota((ROWS, LANES), 1)
    slot = iota((16, LANES), 0)
    half = jnp.zeros((16, LANES), F32)
    for block in range(2):
        for qubit in range(7):
            half = jnp.where(slot == block * 8 + qubit, angles[k, block, qubit] * 0.5, half)
    cosines = jnp.cos(half)
    sines = jnp.sin(half)

    high, low = split(rotation_product(cols, rows, cosines, sines, 0))
    both = jnp.concatenate([high, low], axis=1)
    right_tab[k, 0:ROWS, :] = both
    right_tab[k, ROWS : 2 * ROWS, :] = both

    out = row_order(rows, k, bit)
    inp = jnp.where(k == 0, cols, row_order(cols, before, bit_before))
    high, low = split(rotation_product(out, inp, cosines, sines, 8))
    left_tab[k, 0:ROWS, :] = jnp.concatenate([high, high], axis=1)
    left_tab[k, ROWS : 2 * ROWS, :] = jnp.concatenate([low, low], axis=1)

    def signs(index):
        parity = jnp.zeros(index.shape, jnp.int32)
        for pair in range(12):
            parity = parity ^ ((index >> pairs[k, 0, pair]) & (index >> pairs[k, 1, pair]))
        return (1 - 2 * (parity & 1)).astype(F32)

    sign_tab[k] = signs(out * 128 + cols)
    by_row = signs(out[:, :CHUNKS] * 128 + cols[:, :CHUNKS] * 16384)
    row_tab[k] = (by_row * by_row[:, 0:1]).astype(BF16)
    by_lane = signs(rows[:CHUNKS] * 16384 + cols[:CHUNKS])
    lane_tab[k] = by_lane * by_lane[0:1, :] * by_lane[:, 0:1]


def gates(taken, slot, right_tab, left_tab, sign_tab, row_tab, lane_tab):
    chunk = iota((CHUNKS, LANES), 0)
    sums = {}
    for k in taken:
        high, low = split(taken[k].reshape(GROUP * ROWS, LANES))
        sums[k] = jnp.dot(jnp.concatenate([high, low], axis=1), right_tab[k], preferred_element_type=F32)
    phase = {}
    for k in taken:
        lanes = lane_tab[k]
        picks = [jnp.where(chunk == slot[k] * GROUP + j, lanes, 0.0) for j in range(GROUP)]
        picks = jnp.concatenate(picks, axis=1).astype(BF16)
        phase[k] = jnp.dot(row_tab[k], picks, preferred_element_type=F32)
    for k in taken:
        high, low = split(sums[k][:, :LANES] + sums[k][:, LANES:])
        beside = [
            jnp.concatenate([part[j * ROWS : (j + 1) * ROWS] for j in range(GROUP)], axis=1) for part in (high, low)
        ]
        sums[k] = jnp.dot(left_tab[k], jnp.concatenate(beside, axis=0), preferred_element_type=F32)
    given = {}
    for k in taken:
        total = sums[k][:ROWS] + sums[k][ROWS:]
        sign = sign_tab[k]
        given[k] = [
            total[:, j * LANES : (j + 1) * LANES] * (sign * phase[k][:, j * LANES : (j + 1) * LANES])
            for j in range(GROUP)
        ]
    return given


def kernel(
    angles_in, pairs_in, state, final, angles, pairs, held, leave, right_tab, left_tab, sign_tab, row_tab, lane_tab,
    small_sem, in_sem, out_sem, send_sem, recv_sem
):
    wide = lax.axis_index("wide")
    narrow = lax.axis_index("narrow")
    tables = (right_tab, left_tab, sign_tab, row_tab, lane_tab)

    def fetch(g):
        part = pl.ds(g * GROUP, GROUP)
        return pltpu.make_async_copy(state.at[part], held.at[0, part], in_sem.at[g])

    def trade(k, part, g):
        return pltpu.make_async_remote_copy(
            src_ref=leave.at[k, part],
            dst_ref=held.at[k + 1, part, HALF:ROWS],
            send_sem=send_sem.at[k],
            recv_sem=recv_sem.at[k, g],
            device_id=partner_of(k, wide, narrow),
            device_id_type=MESH,
        )

    def of(g):
        return pl.ds(g * GROUP, GROUP)

    _, last_bit = trade_bit(ROUNDS - 1, wide, narrow)

    def deliver(g, side):
        copies = []
        for upper in range(2):
            begin = side * HALF + upper * 32
            place = upper * HALF + 32 * (last_bit * (1 - 2 * side) + side)
            copies.append(
                pltpu.make_async_copy(
                    held.at[ROUNDS, of(g), begin : begin + 32],
                    final.at[of(g), pl.ds(pl.multiple_of(place, 32), 32)],
                    out_sem,
                )
            )
        return copies

    small = [pltpu.make_async_copy(angles_in, angles, small_sem.at[0]), pltpu.make_async_copy(pairs_in, pairs, small_sem.at[1])]
    for copy in small:
        copy.start()
    barrier = pltpu.get_barrier_semaphore()
    for k in range(ROUNDS):
        pl.semaphore_signal(barrier, inc=1, device_id=partner_of(k, wide, narrow), device_id_type=MESH)

    @pl.loop(0, GROUPS)
    def _(g):
        fetch(g).start()

    for copy in small:
        copy.wait()
    build(jnp.int32(0), wide, narrow, angles, pairs, *tables)
    pl.semaphore_wait(barrier, ROUNDS)

    @pl.loop(0, GROUPS + OFFSET[ROUNDS])
    def _(step):
        for block in BLOCKS:
            at = {k: step - OFFSET[k] for k in block}
            for k in block:
                @pl.when((at[k] >= 0) & (at[k] < GROUPS))
                def _(k=k):
                    if k == 0:
                        fetch(at[k]).wait()
                    else:
                        trade(k - 1, of(at[k]), at[k]).wait_recv()

            slot = {k: jnp.where((at[k] >= 0) & (at[k] < GROUPS), at[k], GROUPS) for k in block}
            taken = {k: held[k, of(slot[k])] for k in block}
            given = gates(taken, slot, *tables)
            for k in block:
                for j in range(GROUP):
                    leave[k, slot[k] * GROUP + j] = given[k][j][HALF:]
                    held[k + 1, slot[k] * GROUP + j, 0:HALF] = given[k][j][:HALF]
            for k in block:
                @pl.when((at[k] >= 0) & (at[k] < GROUPS))
                def _(k=k):
                    trade(k, of(at[k]), at[k]).start()
                    if k == ROUNDS - 1:
                        for copy in deliver(at[k], 0):
                            copy.start()

        @pl.when(step < ROUNDS - 1)
        def _():
            build(jnp.minimum(step + 1, ROUNDS - 1), wide, narrow, angles, pairs, *tables)

        done = step - OFFSET[ROUNDS]

        @pl.when(done >= 0)
        def _():
            trade(ROUNDS - 1, of(done), done).wait_recv()
            for copy in deliver(done, 1):
                copy.start()

    for k in range(ROUNDS):
        trade(k, slice(0, CHUNKS), 0).wait_send()
    pltpu.make_async_copy(held.at[ROUNDS, 0:CHUNKS], final, out_sem).wait()


def body(state, angles, cz_pairs):
    hbm = pl.BlockSpec(memory_space=pltpu.HBM)
    result = pl.pallas_call(
        kernel,
        out_shape=jax.ShapeDtypeStruct((CHUNKS, ROWS, LANES), F32),
        in_specs=[hbm, hbm, hbm],
        out_specs=pl.BlockSpec(memory_space=pl.ANY),
        scratch_shapes=[
            pltpu.SMEM((ROUNDS, 2, 7), F32),
            pltpu.SMEM((ROUNDS, 2, 12), jnp.int32),
            pltpu.VMEM((ROUNDS + 1, CHUNKS + GROUP, ROWS, LANES), F32),
            pltpu.VMEM((ROUNDS, CHUNKS + GROUP, HALF, LANES), F32),
            pltpu.VMEM((ROUNDS, 2 * ROWS, 2 * LANES), BF16),
            pltpu.VMEM((ROUNDS, 2 * ROWS, 2 * LANES), BF16),
            pltpu.VMEM((ROUNDS, ROWS, LANES), F32),
            pltpu.VMEM((ROUNDS, ROWS, CHUNKS), BF16),
            pltpu.VMEM((ROUNDS, CHUNKS, LANES), F32),
            pltpu.SemaphoreType.DMA((2,)),
            pltpu.SemaphoreType.DMA((GROUPS,)),
            pltpu.SemaphoreType.DMA,
            pltpu.SemaphoreType.DMA((ROUNDS,)),
            pltpu.SemaphoreType.DMA((ROUNDS, GROUPS)),
        ],
        compiler_params=pltpu.CompilerParams(
            collective_id=0, has_side_effects=True, vmem_limit_bytes=48 << 20
        ),
        name="circuit",
    )(*[pltpu.with_memory_space_constraint(v, pltpu.HBM) for v in (angles, cz_pairs.transpose(0, 2, 1))], pltpu.with_memory_space_constraint(state.reshape(CHUNKS, ROWS, LANES), pltpu.HBM))
    return result.reshape(state.shape)


def solution(mesh):
    return jax.shard_map(
        body,
        mesh=mesh,
        in_specs=(P("wide", "narrow", None), P(), P()),
        out_specs=P("wide", "narrow", None),
        check_vma=False,
    )
```

time: 93.9 us -> 70.2 us (0.75)
  Pallas kernels: 89.3 us -> 68.4 us
  local copies, waits for them, and re-layouts: 4.41 us -> 1.32 us
    pallas_call x1, Pallas kernels: 89.3 us -> 68.4 us  [body(): pl.pallas_call(kernel, out_shape=jax.ShapeDtypeStruct((CHUNKS, ROWS, LANE...]
    unnamed x6 -> x1, local copies, waits for them, and re-layouts: 4.41 us -> 1.32 us
where the time goes in v1:
time: 70.2 us; the launch traced here: 69.7 us
  Pallas kernels  68.4 us (97%)
  local copies, waits for them, and re-layouts  1.32 us (2%)
    pallas_call x1, Pallas kernels, body(): pl.pallas_call(kernel, out_shape=jax.ShapeDtypeStruct((CHUNKS, ROWS, LANE...  68.4 us

profile of v1, /device:TPU:0, one launch (start us, length us, event | category | flops | bytes accessed | tf_op | source)
XLA Modules:
  0.0 69.7 jit_solution(2925386388690965463)
XLA Ops:
  0.0 68.4 %circuit.1 = f32[32,128,128]{2,1,0:T(8,128)S(1)} custom-call(f32[6,2,7]{2,1,0:T(2,128)} %angles_in.1, s32[6,2,12]{2,1,0:T(2,128)} %bitcast.5, f32[32,128,128]{2,1,0:T(8,128)} %bitcast.4), custom_call_target="tpu_custom_call" | custom-call | tf_op jit(solution)/shard_map/circuit/pallas_call | solution.py:244
  68.4 1.3 %copy.5 = f32[1,1,524288]{2,1,0:T(1,128)} copy(f32[1,1,524288]{2,1,0:T(1,128)S(1)} %bitcast.3) | data formatting | bytes 4194304

commit v2 on v1

--- a/solution.py
+++ b/solution.py
@@ -17,7 +17,8 @@
 CHUNKS = 32
 GROUP = 2
 GROUPS = CHUNKS // GROUP
-OFFSET = (0, 1, 4, 7, 11, 15, 18)
+TWICE = (3, 4)
+OFFSET = (0, 2, 6, 10, 14, 18)
 BLOCKS = (tuple(range(ROUNDS)),)
 
 
@@ -34,8 +35,11 @@
 def partner_of(k, wide, narrow):
     step, bit = trade_bit(k, wide, narrow)
     move = step * (1 - 2 * bit)
-    even = 1 - k % 2
-    return wide + move * even, narrow + move * (1 - even)
+    return (wide, narrow + move) if k % 2 else (wide + move, narrow)
+
+
+def beyond(k, wide, narrow):
+    return partner_of(k, *partner_of(k - 2, wide, narrow))
 
 
 def row_order(pos, k, bit):
@@ -90,7 +94,7 @@
     right_tab[k, 0:ROWS, :] = both
     right_tab[k, ROWS : 2 * ROWS, :] = both
 
-    out = row_order(rows, k, bit)
+    out = row_order(rows, k, bit ^ jnp.where((k == 1) | (k == 2), 1, 0))
     inp = jnp.where(k == 0, cols, row_order(cols, before, bit_before))
     high, low = split(rotation_product(out, inp, cosines, sines, 8))
     left_tab[k, 0:ROWS, :] = jnp.concatenate([high, high], axis=1)
@@ -140,7 +144,7 @@
 
 def kernel(
     angles_in, pairs_in, state, final, angles, pairs, held, leave, right_tab, left_tab, sign_tab, row_tab, lane_tab,
-    small_sem, in_sem, out_sem, send_sem, recv_sem
+    small_sem, in_sem, out_sem, last_sem, send_sem, recv_sem
 ):
     wide = lax.axis_index("wide")
     narrow = lax.axis_index("narrow")
@@ -150,41 +154,63 @@
         part = pl.ds(g * GROUP, GROUP)
         return pltpu.make_async_copy(state.at[part], held.at[0, part], in_sem.at[g])
 
-    def trade(k, part, g):
+    def send(k, part, side, recv, device):
         return pltpu.make_async_remote_copy(
-            src_ref=leave.at[k, part],
-            dst_ref=held.at[k + 1, part, HALF:ROWS],
+            src_ref=leave.at[k, part, side * HALF : (side + 1) * HALF],
+            dst_ref=held.at[k + 1, part, side * HALF : (side + 1) * HALF],
             send_sem=send_sem.at[k],
-            recv_sem=recv_sem.at[k, g],
-            device_id=partner_of(k, wide, narrow),
+            recv_sem=recv,
+            device_id=device,
             device_id_type=MESH,
         )
 
+    def trade(k, g):
+        part, recv = of(g), recv_sem.at[k, g]
+        if k in TWICE:
+            return [
+                send(k, part, 0, recv, partner_of(k - 2, wide, narrow)),
+                send(k, part, 1, recv, beyond(k, wide, narrow)),
+            ]
+        if k < ROUNDS - 1:
+            return [send(k, part, 1, recv, partner_of(k, wide, narrow))]
+        return [
+            pltpu.make_async_remote_copy(
+                src_ref=leave.at[k, part, HALF + 32 * upper : HALF + 32 * upper + 32],
+                dst_ref=final.at[part, pl.ds(pl.multiple_of(upper * HALF + 32 * last_bit, 32), 32)],
+                send_sem=send_sem.at[k],
+                recv_sem=last_sem,
+                device_id=partner_of(k, wide, narrow),
+                device_id_type=MESH,
+            )
+            for upper in range(2)
+        ]
+
+    def arrived(k, g):
+        rows = slice(0, ROWS) if k in TWICE else slice(HALF, ROWS)
+        pltpu.make_async_copy(leave.at[k, of(g), rows], held.at[k + 1, of(g), rows], recv_sem.at[k, g]).wait()
+
     def of(g):
         return pl.ds(g * GROUP, GROUP)
 
     _, last_bit = trade_bit(ROUNDS - 1, wide, narrow)
 
-    def deliver(g, side):
-        copies = []
-        for upper in range(2):
-            begin = side * HALF + upper * 32
-            place = upper * HALF + 32 * (last_bit * (1 - 2 * side) + side)
-            copies.append(
-                pltpu.make_async_copy(
-                    held.at[ROUNDS, of(g), begin : begin + 32],
-                    final.at[of(g), pl.ds(pl.multiple_of(place, 32), 32)],
-                    out_sem,
-                )
+    def deliver(g):
+        return [
+            pltpu.make_async_copy(
+                leave.at[ROUNDS - 1, of(g), 32 * upper : 32 * upper + 32],
+                final.at[of(g), pl.ds(pl.multiple_of(upper * HALF + 32 * last_bit, 32), 32)],
+                out_sem,
             )
-        return copies
+            for upper in range(2)
+        ]
 
     small = [pltpu.make_async_copy(angles_in, angles, small_sem.at[0]), pltpu.make_async_copy(pairs_in, pairs, small_sem.at[1])]
     for copy in small:
         copy.start()
     barrier = pltpu.get_barrier_semaphore()
     for k in range(ROUNDS):
-        pl.semaphore_signal(barrier, inc=1, device_id=partner_of(k, wide, narrow), device_id_type=MESH)
+        greeted = beyond(k, wide, narrow) if k in TWICE else partner_of(k, wide, narrow)
+        pl.semaphore_signal(barrier, inc=1, device_id=greeted, device_id_type=MESH)
 
     @pl.loop(0, GROUPS)
     def _(g):
@@ -193,9 +219,8 @@
     for copy in small:
         copy.wait()
     build(jnp.int32(0), wide, narrow, angles, pairs, *tables)
-    pl.semaphore_wait(barrier, ROUNDS)
-
-    @pl.loop(0, GROUPS + OFFSET[ROUNDS])
+
+    @pl.loop(0, GROUPS + OFFSET[ROUNDS - 1])
     def _(step):
         for block in BLOCKS:
             at = {k: step - OFFSET[k] for k in block}
@@ -205,38 +230,40 @@
                     if k == 0:
                         fetch(at[k]).wait()
                     else:
-                        trade(k - 1, of(at[k]), at[k]).wait_recv()
+                        arrived(k - 1, at[k])
 
             slot = {k: jnp.where((at[k] >= 0) & (at[k] < GROUPS), at[k], GROUPS) for k in block}
             taken = {k: held[k, of(slot[k])] for k in block}
             given = gates(taken, slot, *tables)
             for k in block:
                 for j in range(GROUP):
-                    leave[k, slot[k] * GROUP + j] = given[k][j][HALF:]
-                    held[k + 1, slot[k] * GROUP + j, 0:HALF] = given[k][j][:HALF]
+                    if k in TWICE or k == ROUNDS - 1:
+                        leave[k, slot[k] * GROUP + j] = given[k][j]
+                    else:
+                        leave[k, slot[k] * GROUP + j, HALF:ROWS] = given[k][j][HALF:]
+                        held[k + 1, slot[k] * GROUP + j, 0:HALF] = given[k][j][:HALF]
+            if 0 in block:
+                @pl.when(step == 0)
+                def _():
+                    pl.semaphore_wait(barrier, ROUNDS)
+
             for k in block:
                 @pl.when((at[k] >= 0) & (at[k] < GROUPS))
                 def _(k=k):
-                    trade(k, of(at[k]), at[k]).start()
-                    if k == ROUNDS - 1:
-                        for copy in deliver(at[k], 0):
-                            copy.start()
+                    for copy in trade(k, at[k]) + (deliver(at[k]) if k == ROUNDS - 1 else []):
+                        copy.start()
 
         @pl.when(step < ROUNDS - 1)
         def _():
             build(jnp.minimum(step + 1, ROUNDS - 1), wide, narrow, angles, pairs, *tables)
 
-        done = step - OFFSET[ROUNDS]
-
-        @pl.when(done >= 0)
-        def _():
-            trade(ROUNDS - 1, of(done), done).wait_recv()
-            for copy in deliver(done, 1):
-                copy.start()
-
     for k in range(ROUNDS):
-        trade(k, slice(0, CHUNKS), 0).wait_send()
-    pltpu.make_async_copy(held.at[ROUNDS, 0:CHUNKS], final, out_sem).wait()
+        rows = slice(0, ROWS) if k in TWICE else slice(HALF, ROWS)
+        sent = leave.at[k, 0:CHUNKS, rows]
+        pltpu.make_async_copy(sent, sent, send_sem.at[k]).wait()
+    lower = leave.at[ROUNDS - 1, 0:CHUNKS, 0:HALF]
+    pltpu.make_async_copy(lower, lower, out_sem).wait()
+    pltpu.make_async_copy(lower, lower, last_sem).wait()
 
 
 def body(state, angles, cz_pairs):
@@ -249,8 +276,8 @@
         scratch_shapes=[
             pltpu.SMEM((ROUNDS, 2, 7), F32),
             pltpu.SMEM((ROUNDS, 2, 12), jnp.int32),
-            pltpu.VMEM((ROUNDS + 1, CHUNKS + GROUP, ROWS, LANES), F32),
-            pltpu.VMEM((ROUNDS, CHUNKS + GROUP, HALF, LANES), F32),
+            pltpu.VMEM((ROUNDS, CHUNKS + GROUP, ROWS, LANES), F32),
+            pltpu.VMEM((ROUNDS, CHUNKS + GROUP, ROWS, LANES), F32),
             pltpu.VMEM((ROUNDS, 2 * ROWS, 2 * LANES), BF16),
             pltpu.VMEM((ROUNDS, 2 * ROWS, 2 * LANES), BF16),
             pltpu.VMEM((ROUNDS, ROWS, LANES), F32),
@@ -259,8 +286,9 @@
             pltpu.SemaphoreType.DMA((2,)),
             pltpu.SemaphoreType.DMA((GROUPS,)),
             pltpu.SemaphoreType.DMA,
+            pltpu.SemaphoreType.DMA,
             pltpu.SemaphoreType.DMA((ROUNDS,)),
-            pltpu.SemaphoreType.DMA((ROUNDS, GROUPS)),
+            pltpu.SemaphoreType.DMA((ROUNDS - 1, GROUPS)),
         ],
         compiler_params=pltpu.CompilerParams(
             collective_id=0, has_side_effects=True, vmem_limit_bytes=48 << 20

time: 70.2 us -> 66.2 us (0.943)
  Pallas kernels: 68.4 us -> 64.8 us
    pallas_call x1, Pallas kernels: 68.4 us -> 64.8 us  [body(): pl.pallas_call(kernel, out_shape=jax.ShapeDtypeStruct((CHUNKS, ROWS, LANE...]
where the time goes in v2:
time: 66.2 us; the launch traced here: 66.1 us
  Pallas kernels  64.8 us (98%)
  local copies, waits for them, and re-layouts  1.32 us (2%)
    pallas_call x1, Pallas kernels, body(): pl.pallas_call(kernel, out_shape=jax.ShapeDtypeStruct((CHUNKS, ROWS, LANE...  64.8 us

profile of v2, /device:TPU:0, one launch (start us, length us, event | category | flops | bytes accessed | tf_op | source)
XLA Modules:
  0.0 66.1 jit_solution(4673703758441952222)
XLA Ops:
  0.0 64.8 %circuit.1 = f32[32,128,128]{2,1,0:T(8,128)S(1)} custom-call(f32[6,2,7]{2,1,0:T(2,128)} %angles_in.1, s32[6,2,12]{2,1,0:T(2,128)} %bitcast.5, f32[32,128,128]{2,1,0:T(8,128)} %bitcast.4), custom_call_target="tpu_custom_call" | custom-call | tf_op jit(solution)/shard_map/circuit/pallas_call | solution.py:271
  64.8 1.3 %copy.5 = f32[1,1,524288]{2,1,0:T(1,128)} copy(f32[1,1,524288]{2,1,0:T(1,128)S(1)} %bitcast.3) | data formatting | bytes 4194304

commit v3 on v2

--- a/solution.py
+++ b/solution.py
@@ -15,20 +15,16 @@
 LANES = 128
 HALF = 64
 CHUNKS = 32
-GROUP = 2
+GROUP = 1
 GROUPS = CHUNKS // GROUP
 TWICE = (3, 4)
-OFFSET = (0, 2, 6, 10, 14, 18)
-BLOCKS = (tuple(range(ROUNDS)),)
+OFFSET = (0, 2, 8, 14, 20, 26)
+ORDER = (0, 1, 2, 3, 4, 5)
+BUILD = (0, 1, 8, 14, 20, 26)
 
 
 def trade_bit(k, wide, narrow):
-    level = k // 2
-    if isinstance(k, int):
-        step, index = 1 << level, (narrow if k % 2 else wide)
-    else:
-        step = jnp.where(level == 0, 1, jnp.where(level == 1, 2, 4))
-        index = jnp.where(k % 2 == 0, wide, narrow)
+    step, index = 1 << k // 2, (narrow if k % 2 else wide)
     return step, (index // step) % 2
 
 
@@ -77,8 +73,6 @@
 
 def build(k, wide, narrow, angles, pairs, right_tab, left_tab, sign_tab, row_tab, lane_tab):
     _, bit = trade_bit(k, wide, narrow)
-    before = jnp.maximum(k - 1, 0)
-    _, bit_before = trade_bit(before, wide, narrow)
     rows = iota((ROWS, LANES), 0)
     cols = iota((ROWS, LANES), 1)
     slot = iota((16, LANES), 0)
@@ -94,8 +88,8 @@
     right_tab[k, 0:ROWS, :] = both
     right_tab[k, ROWS : 2 * ROWS, :] = both
 
-    out = row_order(rows, k, bit ^ jnp.where((k == 1) | (k == 2), 1, 0))
-    inp = jnp.where(k == 0, cols, row_order(cols, before, bit_before))
+    out = row_order(rows, k, bit ^ (1 if k in (1, 2) else 0))
+    inp = row_order(cols, k - 1, trade_bit(k - 1, wide, narrow)[1]) if k else cols
     high, low = split(rotation_product(out, inp, cosines, sines, 8))
     left_tab[k, 0:ROWS, :] = jnp.concatenate([high, high], axis=1)
     left_tab[k, ROWS : 2 * ROWS, :] = jnp.concatenate([low, low], axis=1)
@@ -218,44 +212,36 @@
 
     for copy in small:
         copy.wait()
-    build(jnp.int32(0), wide, narrow, angles, pairs, *tables)
-
-    @pl.loop(0, GROUPS + OFFSET[ROUNDS - 1])
-    def _(step):
-        for block in BLOCKS:
+    build(0, wide, narrow, angles, pairs, *tables)
+    edges = sorted({OFFSET[k] + e for k in range(ROUNDS) for e in (0, GROUPS)} | {1})
+    for begin, end in zip(edges[:-1], edges[1:]):
+        block = [k for k in ORDER if OFFSET[k] <= begin and end <= OFFSET[k] + GROUPS]
+
+        @pl.loop(begin, end)
+        def _(step):
             at = {k: step - OFFSET[k] for k in block}
             for k in block:
-                @pl.when((at[k] >= 0) & (at[k] < GROUPS))
-                def _(k=k):
-                    if k == 0:
-                        fetch(at[k]).wait()
-                    else:
-                        arrived(k - 1, at[k])
-
-            slot = {k: jnp.where((at[k] >= 0) & (at[k] < GROUPS), at[k], GROUPS) for k in block}
-            taken = {k: held[k, of(slot[k])] for k in block}
-            given = gates(taken, slot, *tables)
+                if k == 0:
+                    fetch(at[k]).wait()
+                else:
+                    arrived(k - 1, at[k])
+            given = gates({k: held[k, of(at[k])] for k in block}, at, *tables)
             for k in block:
                 for j in range(GROUP):
                     if k in TWICE or k == ROUNDS - 1:
-                        leave[k, slot[k] * GROUP + j] = given[k][j]
+                        leave[k, at[k] * GROUP + j] = given[k][j]
                     else:
-                        leave[k, slot[k] * GROUP + j, HALF:ROWS] = given[k][j][HALF:]
-                        held[k + 1, slot[k] * GROUP + j, 0:HALF] = given[k][j][:HALF]
-            if 0 in block:
-                @pl.when(step == 0)
-                def _():
-                    pl.semaphore_wait(barrier, ROUNDS)
-
+                        leave[k, at[k] * GROUP + j, HALF:ROWS] = given[k][j][HALF:]
+                        held[k + 1, at[k] * GROUP + j, 0:HALF] = given[k][j][:HALF]
+            if begin == 0:
+                pl.semaphore_wait(barrier, ROUNDS)
             for k in block:
-                @pl.when((at[k] >= 0) & (at[k] < GROUPS))
-                def _(k=k):
-                    for copy in trade(k, at[k]) + (deliver(at[k]) if k == ROUNDS - 1 else []):
-                        copy.start()
-
-        @pl.when(step < ROUNDS - 1)
-        def _():
-            build(jnp.minimum(step + 1, ROUNDS - 1), wide, narrow, angles, pairs, *tables)
+                for copy in trade(k, at[k]) + (deliver(at[k]) if k == ROUNDS - 1 else []):
+                    copy.start()
+
+        for k in range(1, ROUNDS):
+            if BUILD[k] == end:
+                build(k, wide, narrow, angles, pairs, *tables)
 
     for k in range(ROUNDS):
         rows = slice(0, ROWS) if k in TWICE else slice(HALF, ROWS)
@@ -276,8 +262,8 @@
         scratch_shapes=[
             pltpu.SMEM((ROUNDS, 2, 7), F32),
             pltpu.SMEM((ROUNDS, 2, 12), jnp.int32),
-            pltpu.VMEM((ROUNDS, CHUNKS + GROUP, ROWS, LANES), F32),
-            pltpu.VMEM((ROUNDS, CHUNKS + GROUP, ROWS, LANES), F32),
+            pltpu.VMEM((ROUNDS, CHUNKS, ROWS, LANES), F32),
+            pltpu.VMEM((ROUNDS, CHUNKS, ROWS, LANES), F32),
             pltpu.VMEM((ROUNDS, 2 * ROWS, 2 * LANES), BF16),
             pltpu.VMEM((ROUNDS, 2 * ROWS, 2 * LANES), BF16),
             pltpu.VMEM((ROUNDS, ROWS, LANES), F32),

time: 66.2 us -> 64.8 us (0.979)
  Pallas kernels: 64.8 us -> 63.3 us
    pallas_call x1, Pallas kernels: 64.8 us -> 63.3 us  [body(): pl.pallas_call(kernel, out_shape=jax.ShapeDtypeStruct((CHUNKS, ROWS, LANE...]
where the time goes in v3:
time: 64.8 us; the launch traced here: 64.6 us
  Pallas kernels  63.3 us (98%)
  local copies, waits for them, and re-layouts  1.32 us (2%)
    pallas_call x1, Pallas kernels, body(): pl.pallas_call(kernel, out_shape=jax.ShapeDtypeStruct((CHUNKS, ROWS, LANE...  63.3 us
    unnamed x1, local copies, waits for them, and re-layouts  1.32 us

profile of v3, /device:TPU:0, one launch (start us, length us, event | category | flops | bytes accessed | tf_op | source)
XLA Modules:
  0.0 64.6 jit_solution(7983859933925556929)
XLA Ops:
  0.0 63.3 %circuit.1 = f32[32,128,128]{2,1,0:T(8,128)S(1)} custom-call(f32[6,2,7]{2,1,0:T(2,128)} %angles_in.1, s32[6,2,12]{2,1,0:T(2,128)} %bitcast.5, f32[32,128,128]{2,1,0:T(8,128)} %bitcast.4), custom_call_target="tpu_custom_call" | custom-call | tf_op jit(solution)/shard_map/circuit/pallas_call | solution.py:257
  63.3 1.3 %copy.5 = f32[1,1,524288]{2,1,0:T(1,128)} copy(f32[1,1,524288]{2,1,0:T(1,128)S(1)} %bitcast.3) | data formatting | bytes 4194304

commit v4 on v3

--- a/solution.py
+++ b/solution.py
@@ -18,9 +18,9 @@
 GROUP = 1
 GROUPS = CHUNKS // GROUP
 TWICE = (3, 4)
-OFFSET = (0, 2, 8, 14, 20, 26)
+OFFSET = (0, 3, 9, 15, 21, 27)
 ORDER = (0, 1, 2, 3, 4, 5)
-BUILD = (0, 1, 8, 14, 20, 26)
+BUILD = (0, 1, 9, 15, 21, 27)
 
 
 def trade_bit(k, wide, narrow):
@@ -137,7 +137,7 @@
 
 
 def kernel(
-    angles_in, pairs_in, state, final, angles, pairs, held, leave, right_tab, left_tab, sign_tab, row_tab, lane_tab,
+    angles_in, pairs_in, state, final, angles, pairs, held, leave, result, right_tab, left_tab, sign_tab, row_tab, lane_tab,
     small_sem, in_sem, out_sem, last_sem, send_sem, recv_sem
 ):
     wide = lax.axis_index("wide")
@@ -169,14 +169,13 @@
             return [send(k, part, 1, recv, partner_of(k, wide, narrow))]
         return [
             pltpu.make_async_remote_copy(
-                src_ref=leave.at[k, part, HALF + 32 * upper : HALF + 32 * upper + 32],
-                dst_ref=final.at[part, pl.ds(pl.multiple_of(upper * HALF + 32 * last_bit, 32), 32)],
+                src_ref=result.at[part, 1],
+                dst_ref=final.at[part, :, last_bit],
                 send_sem=send_sem.at[k],
                 recv_sem=last_sem,
                 device_id=partner_of(k, wide, narrow),
                 device_id_type=MESH,
             )
-            for upper in range(2)
         ]
 
     def arrived(k, g):
@@ -189,14 +188,7 @@
     _, last_bit = trade_bit(ROUNDS - 1, wide, narrow)
 
     def deliver(g):
-        return [
-            pltpu.make_async_copy(
-                leave.at[ROUNDS - 1, of(g), 32 * upper : 32 * upper + 32],
-                final.at[of(g), pl.ds(pl.multiple_of(upper * HALF + 32 * last_bit, 32), 32)],
-                out_sem,
-            )
-            for upper in range(2)
-        ]
+        return [pltpu.make_async_copy(result.at[of(g), 0], final.at[of(g), :, last_bit], out_sem)]
 
     small = [pltpu.make_async_copy(angles_in, angles, small_sem.at[0]), pltpu.make_async_copy(pairs_in, pairs, small_sem.at[1])]
     for copy in small:
@@ -228,7 +220,9 @@
             given = gates({k: held[k, of(at[k])] for k in block}, at, *tables)
             for k in block:
                 for j in range(GROUP):
-                    if k in TWICE or k == ROUNDS - 1:
+                    if k == ROUNDS - 1:
+                        result[at[k] * GROUP + j] = given[k][j].reshape(2, 2, 32, LANES)
+                    elif k in TWICE:
                         leave[k, at[k] * GROUP + j] = given[k][j]
                     else:
                         leave[k, at[k] * GROUP + j, HALF:ROWS] = given[k][j][HALF:]
@@ -243,27 +237,27 @@
             if BUILD[k] == end:
                 build(k, wide, narrow, angles, pairs, *tables)
 
-    for k in range(ROUNDS):
+    for k in range(ROUNDS - 1):
         rows = slice(0, ROWS) if k in TWICE else slice(HALF, ROWS)
         sent = leave.at[k, 0:CHUNKS, rows]
         pltpu.make_async_copy(sent, sent, send_sem.at[k]).wait()
-    lower = leave.at[ROUNDS - 1, 0:CHUNKS, 0:HALF]
-    pltpu.make_async_copy(lower, lower, out_sem).wait()
-    pltpu.make_async_copy(lower, lower, last_sem).wait()
+    for semaphore in (send_sem.at[ROUNDS - 1], out_sem, last_sem):
+        pltpu.make_async_copy(result.at[:, 0], result.at[:, 1], semaphore).wait()
 
 
 def body(state, angles, cz_pairs):
     hbm = pl.BlockSpec(memory_space=pltpu.HBM)
-    result = pl.pallas_call(
+    ended = pl.pallas_call(
         kernel,
-        out_shape=jax.ShapeDtypeStruct((CHUNKS, ROWS, LANES), F32),
+        out_shape=jax.ShapeDtypeStruct((CHUNKS, 2, 2, 32, LANES), F32),
         in_specs=[hbm, hbm, hbm],
         out_specs=pl.BlockSpec(memory_space=pl.ANY),
         scratch_shapes=[
             pltpu.SMEM((ROUNDS, 2, 7), F32),
             pltpu.SMEM((ROUNDS, 2, 12), jnp.int32),
             pltpu.VMEM((ROUNDS, CHUNKS, ROWS, LANES), F32),
-            pltpu.VMEM((ROUNDS, CHUNKS, ROWS, LANES), F32),
+            pltpu.VMEM((ROUNDS - 1, CHUNKS, ROWS, LANES), F32),
+            pltpu.VMEM((CHUNKS, 2, 2, 32, LANES), F32),
             pltpu.VMEM((ROUNDS, 2 * ROWS, 2 * LANES), BF16),
             pltpu.VMEM((ROUNDS, 2 * ROWS, 2 * LANES), BF16),
             pltpu.VMEM((ROUNDS, ROWS, LANES), F32),
@@ -281,7 +275,7 @@
         ),
         name="circuit",
     )(*[pltpu.with_memory_space_constraint(v, pltpu.HBM) for v in (angles, cz_pairs.transpose(0, 2, 1))], pltpu.with_memory_space_constraint(state.reshape(CHUNKS, ROWS, LANES), pltpu.HBM))
-    return result.reshape(state.shape)
+    return ended.reshape(state.shape)
 
 
 def solution(mesh):

time: 64.8 us -> 64.6 us (level)
  no operation moved by 1% of the time
where the time goes in v4:
time: 64.6 us; the launch traced here: 64.3 us
  Pallas kernels  63 us (98%)
  local copies, waits for them, and re-layouts  1.32 us (2%)
    pallas_call x1, Pallas kernels, body(): pl.pallas_call(kernel, out_shape=jax.ShapeDtypeStruct((CHUNKS, 2, 2, 32,...  63 us
    unnamed x1, local copies, waits for them, and re-layouts  1.32 us

profile of v4, /device:TPU:0, one launch (start us, length us, event | category | flops | bytes accessed | tf_op | source)
XLA Modules:
  0.0 64.3 jit_solution(9058973428424866076)
XLA Ops:
  0.0 63.0 %circuit.1 = f32[32,2,2,32,128]{4,3,2,1,0:T(8,128)S(1)} custom-call(f32[6,2,7]{2,1,0:T(2,128)} %angles_in.1, s32[6,2,12]{2,1,0:T(2,128)} %bitcast.5, f32[32,128,128]{2,1,0:T(8,128)} %bitcast.4), custom_call_target="tpu_custom_call" | custom-call | tf_op jit(solution)/shard_map/circuit/pallas_call | solution.py:250
  63.0 1.3 %copy.5 = f32[1,1,524288]{2,1,0:T(1,128)} copy(f32[1,1,524288]{2,1,0:T(1,128)S(1)} %bitcast.3) | data formatting | bytes 4194304
